TPU v7x, 512 devices: a whole 4x8x8 slice. The times are simulated.
512 devices in a mesh: wide: 64 (over z_lo, y, core), narrow: 8 (over x, z_hi).
Axes of the slice: x: 4, y: 8, z: 8 (z_hi: 2, z_lo: 4; z = z_hi * 4 + z_lo), core: 2. Of those that a mesh axis runs over, the one named last changes fastest.
Arguments:
- features: bfloat16 [16, 1024, 2, 1024], P(None, 'wide', None, 'narrow'), may hold values from -6 to 6
- cotangent: bfloat16 [16, 1024, 2, 1024], P(None, 'wide', None, 'narrow'), may hold values from -6 to 6
- coarse_weight: bfloat16 [32, 16, 3, 3, 3], replicated, may hold values from -0.3125 to 0.3125
- fine_weight: bfloat16 [16, 48, 3, 3, 3], replicated, may hold values from -0.15625 to 0.15625
Outputs:
- output: bfloat16 [16, 1024, 2, 1024], P(None, 'wide', None, 'narrow')
- grad_features: bfloat16 [16, 1024, 2, 1024], P(None, 'wide', None, 'narrow')
- grad_fine: float32 [16, 48, 3, 3, 3], replicated
- grad_coarse: float32 [32, 16, 3, 3, 3], replicated
All inputs are finite; a program needn't handle non-finite values.
Results may differ from a plain program's by a relative error of at most 0.012.
Values may be sent and summed in bfloat16 or wider, within the bound.
A program may use at most 64 MiB of HBM per device.

v0:
```python
import math
import jax
import jax.numpy as jnp
from jax import lax
from jax.sharding import PartitionSpec as P


def extended_2(array, sides, width):
    for axis, dim in sides:
        count, length = (lax.axis_size(axis), array.shape[dim])
        up = [(i, (i + 1) % count) for i in range(count - 1)]
        down = [(j, i) for i, j in up]
        last = lax.slice_in_dim(array, length - width, length, axis=dim)
        first = lax.slice_in_dim(array, 0, width, axis=dim)
        before = lax.ppermute(last, axis, up)
        after = lax.ppermute(first, axis, down)
        array = jnp.concatenate([before, array, after], axis=dim)
    return array


def shortened(array):
    return jax.tree.map(lambda a: a.astype(jnp.bfloat16) if a.dtype == jnp.float32 else a, array)


def correlate(padded, kernel):
    result = lax.conv_general_dilated(
        padded[None],
        kernel,
        (1, 1, 1),
        "VALID",
        dimension_numbers=("NCHWD", "OIHWD", "NCHWD"),
        preferred_element_type=jnp.float32,
    )
    return result[0]


def weight_grad(padded, grad):
    result = lax.conv_general_dilated(
        padded[:, None],
        grad[:, None],
        (1, 1, 1),
        "VALID",
        dimension_numbers=("NCHWD", "OIHWD", "NCHWD"),
        preferred_element_type=jnp.float32,
    )
    return jnp.transpose(result, (1, 0, 2, 3, 4))


def flipped(kernel):
    return jnp.transpose(kernel[:, :, ::-1, ::-1, ::-1], (1, 0, 2, 3, 4))


def pool_sum(field):
    chans, rows, planes, cols = field.shape
    return field.reshape(chans, rows // 2, 2, planes // 2, 2, cols // 2, 2).sum(axis=(2, 4, 6))


def upsample(field):
    chans, rows, planes, cols = field.shape
    spread = jnp.broadcast_to(
        field[:, :, None, :, None, :, None], (chans, rows, 2, planes, 2, cols, 2)
    )
    return spread.reshape(chans, 2 * rows, 2 * planes, 2 * cols)


def silu_slope(value):
    sig = jax.nn.sigmoid(value)
    return sig * (1.0 + value * (1.0 - sig))


def fine_padded(field):
    extended = extended_2(field, (("wide", 1), ("narrow", 3)), 1)
    return jnp.pad(extended, ((0, 0), (0, 0), (1, 1), (0, 0)))


def coarse_padded(field):
    extended = extended_2(field, ((("wide", "narrow"), 1),), 1)
    return jnp.pad(extended, ((0, 0), (0, 0), (1, 1), (1, 1)))


def into_coarse(field):
    return jax.tree.map(
        lambda part, own: part.astype(own.dtype),
        lax.all_to_all(shortened(field), "narrow", split_axis=1, concat_axis=3, tiled=True),
        field,
    )


def into_fine(field):
    return jax.tree.map(
        lambda part, own: part.astype(own.dtype),
        lax.all_to_all(shortened(field), "narrow", split_axis=3, concat_axis=1, tiled=True),
        field,
    )


def shards(features, cotangent, coarse_weight, fine_weight):
    channels = features.shape[0]
    pooled = (pool_sum(features.astype(jnp.float32)) / 8.0).astype(jnp.bfloat16)
    coarse_ext = coarse_padded(into_coarse(pooled))
    coarse_pre = correlate(coarse_ext, coarse_weight)
    coarse_act = jax.nn.silu(coarse_pre).astype(jnp.bfloat16)
    upsampled = upsample(into_fine(coarse_act))
    joined_ext = fine_padded(jnp.concatenate([features, upsampled], 0))
    cotangent_ext = fine_padded(cotangent)
    output = correlate(joined_ext, fine_weight).astype(jnp.bfloat16)
    local_fine = weight_grad(joined_ext, cotangent)
    grad_joined = correlate(cotangent_ext, flipped(fine_weight))
    grad_act = into_coarse(pool_sum(grad_joined[channels:]).astype(jnp.bfloat16))
    grad_pre = (grad_act.astype(jnp.float32) * silu_slope(coarse_pre)).astype(jnp.bfloat16)
    local_coarse = weight_grad(coarse_ext, grad_pre)
    grad_pooled = correlate(coarse_padded(grad_pre), flipped(coarse_weight)).astype(jnp.bfloat16)
    grad_features = (
        grad_joined[:channels] + upsample(into_fine(grad_pooled)).astype(jnp.float32) / 8.0
    ).astype(jnp.bfloat16)
    fine_total, coarse_total = lax.psum((local_fine, local_coarse), ("wide", "narrow"))
    all_cells = (
        features.shape[1]
        * features.shape[2]
        * features.shape[3]
        * lax.axis_size("wide")
        * lax.axis_size("narrow")
    )
    return (
        output,
        grad_features,
        fine_total / math.sqrt(all_cells),
        coarse_total / math.sqrt(all_cells // 8),
    )


def solution(mesh):
    placed = (P(None, "wide", None, "narrow"), P(None, "wide", None, "narrow"), P(), P())
    return jax.shard_map(
        shards,
        mesh=mesh,
        in_specs=placed,
        out_specs=(P(None, "wide", None, "narrow"), P(None, "wide", None, "narrow"), P(), P()),
        check_vma=False,
    )
```

profile of v0, /device:TPU:1, one launch (start us, length us, event | category | flops | bytes accessed | tf_op | source)
XLA Modules:
  0.0 639.0 jit_solution(16950988302908629010)
XLA Ops:
  7.2 0.8 fusion.97
  8.0 4.6 collective-permute-start.6
  12.6 5.5 collective-permute-start.7
  18.1 1.3 convert_reduce_fusion
  19.7 0.9 reduce_sum.25
  21.0 1.3 collective-permute-start.9
  22.3 8.1 %collective-permute-start.8 = (bf16[16,18,2,1]{3,2,1,0:T(2,128)(2,1)S(1)}, bf16[16,18,2,1]{3,2,1,0:T(2,128)(2,1)S(1)}, u32[]{:S(2)}, u32[]{:S(2)}) collective-permute-start(bf16[16,18,2,1]{3,2,1,0:T(2,128)(2,1)S(1)} %get-tuple-element.36), channel_id=1, source_target_pairs={{0,1},{1,2},{2,3},{3,4},{4,5},{5,6},{6,7},{8,9},{9,10},{10,11},{11... | collective-permute-start | bytes 3464 | tf_op jit(solution)/shard_map/ppermute | solution.py:15
  30.6 0.7 reshape.289
  31.3 10.0 %all-to-all-start = ((bf16[8,2,512]{2,1,0:T(2,128)(2,1)}), bf16[8,2,512]{2,1,0:T(2,128)(2,1)S(1)}, u32[]{:S(2)}, u32[]{:S(2)}) async-start(bf16[8,2,512]{2,1,0:T(2,128)(2,1)} %reshape.289), calls=%async_computation | async-start | bytes 32768 | tf_op jit(solution)/shard_map/all_to_all | solution.py:84
  41.3 3.8 copy.231
  45.1 1.3 fusion.54
  46.7 1.8 reshape.286
  48.5 5.1 copy.219
  53.6 1.0 slice.64
  54.7 5.0 fusion.26
  60.4 2.0 copy.221
  62.6 8.5 %collective-permute-start.1 = (bf16[16,1,1,512]{3,0,2,1:T(8,128)(2,1)S(1)}, bf16[16,1,1,512]{3,0,2,1:T(8,128)(2,1)S(1)}, u32[]{:S(2)}, u32[]{:S(2)}) collective-permute-start(bf16[16,1,1,512]{3,0,2,1:T(8,128)(2,1)S(1)} %all_to_all.11), channel_id=1, source_target_pairs={{1,0},{2,1},{3,2},{4,3},{5,4},{6,5},{7,6},{8,7},{9,8},{10,9},{11,1... | collective-permute-start | bytes 49160 | tf_op jit(solution)/shard_map/ppermute | solution.py:16
  71.1 2.1 collective-permute-start
  73.2 1.9 slice_reduce_fusion
  75.1 1.8 reduce_sum.37
  76.9 1.0 copy.222
  77.9 0.7 reshape.287
  78.6 10.8 %all-to-all-start.2 = ((bf16[8,2,1024]{2,1,0:T(2,128)(2,1)}), bf16[8,2,1024]{2,1,0:T(2,128)(2,1)S(1)}, u32[]{:S(2)}, u32[]{:S(2)}) async-start(bf16[8,2,1024]{2,1,0:T(2,128)(2,1)} %reshape.287), calls=%async_computation.2 | async-start | bytes 65536 | tf_op jit(solution)/shard_map/all_to_all | solution.py:84
  89.4 2.8 copy.220
  92.2 2.8 reshape.252
  95.0 0.8 fusion.98
  96.1 0.8 copy.204
  97.0 1.2 fusion.46
  98.2 0.8 fusion.99
  99.3 2.0 copy.233
  101.6 8.2 %collective-permute-start.11 = (bf16[32,1,1,512]{3,0,2,1:T(8,128)(2,1)S(1)}, bf16[32,1,1,512]{3,0,2,1:T(8,128)(2,1)S(1)}, u32[]{:S(2)}, u32[]{:S(2)}) collective-permute-start(bf16[32,1,1,512]{3,0,2,1:T(8,128)(2,1)S(1)} %get-tuple-element.40), channel_id=1, source_target_pairs={{1,0},{2,1},{3,2},{4,3},{5,4},{6,5},{7,6},{8,7},{9,8},{10,9},{11,1... | collective-permute-start | bytes 98312 | tf_op jit(solution)/shard_map/ppermute | solution.py:16
  109.7 1.9 collective-permute-start.10
  112.4 1.5 reduce.8
  113.9 0.8 reshape.291
  114.7 11.2 %all-to-all-start.1 = ((bf16[8,2,1024]{2,1,0:T(2,128)(2,1)}), bf16[8,2,1024]{2,1,0:T(2,128)(2,1)S(1)}, u32[]{:S(2)}, u32[]{:S(2)}) async-start(bf16[8,2,1024]{2,1,0:T(2,128)(2,1)} %reshape.291), calls=%async_computation.1 | async-start | bytes 65536 | tf_op jit(solution)/shard_map/all_to_all | solution.py:92
  126.1 5.7 fusion.101
  131.8 105.8 %psum.15 = f32[32,16,3,3,3]{0,1,4,3,2:T(8,128)S(1)} all-reduce(f32[32,16,3,3,3]{0,1,4,3,2:T(8,128)S(1)} %fusion.101), channel_id=1, replica_groups=mesh['wide'=64,'narrow'=8] {'wide','narrow'}, use_global_device_ids=true, to_apply=%region_5.6 | all-reduce | flops 13824 | bytes 110592 | tf_op jit(solution)/shard_map/psum | solution.py:116
  237.6 0.7 broadcast_multiply_fusion
  239.0 1.7 copy.225
  240.8 1.1 fusion.33
  242.3 1.5 reduce.9
  243.8 0.8 reshape.293
  244.6 3.3 all-to-all-start.3
  248.9 2.9 collective-permute-start.3
  251.8 2.6 collective-permute-start.2
  254.4 2.4 all-to-all-done.3
  258.3 1.3 collective-permute-start.5
  259.6 8.3 %collective-permute-start.4 = (bf16[48,18,2,1]{3,0,2,1:T(8,128)(2,1)S(1)}, bf16[48,18,2,1]{3,0,2,1:T(8,128)(2,1)S(1)}, u32[]{:S(2)}, u32[]{:S(2)}) collective-permute-start(bf16[48,18,2,1]{3,0,2,1:T(8,128)(2,1)S(1)} %get-tuple-element.32), channel_id=1, source_target_pairs={{0,1},{1,2},{2,3},{3,4},{4,5},{5,6},{6,7},{8,9},{9,10},{10,11},{11... | collective-permute-start | bytes 10376 | tf_op jit(solution)/shard_map/ppermute | solution.py:15
  268.0 0.8 copy.236
  268.7 5.5 collective-permute-done.5
  274.2 0.9 collective-permute-done.4
  275.2 0.8 copy-done.1
  275.9 2.0 fusion.111
  277.9 4.9 copy.240
  282.8 1.3 pad.22.clone
  284.5 6.5 %fusion.9 = bf16[16,2,8,17,16]{4,2,3,1,0:T(8,128)(2,1)} fusion(bf16[16,48,3,3,3]{1,0,4,3,2:T(8,128)(2,1)S(1)} %copy-done, bf16[48,18,4,1,7,2]{0,4,5,2,1,3:T(8,128)(2,1)S(1)} %slice.60, bf16[48,18,4,1,8,17]{0,4,5,2,1,3:T(8,128)(2,1)S(1)} %copy.213), kind=kOutput, calls=%fused_computation.12 | convolution fusion | flops 183638016 | bytes 1217536 | tf_op jit(solution)/shard_map/conv_general_dilated | solution.py:26
  291.0 2.7 copy.214
  294.4 0.7 reshape.245
  295.1 1.1 fusion.110
  296.2 8.8 %copy.230 = bf16[48,1,18,4,130]{0,1,4,3,2:T(2,128)(2,1)} copy(bf16[48,1,18,4,130]{4,0,3,2,1:T(8,128)(2,1)S(1)} %fusion.110) | data formatting | bytes 1797120 | tf_op jit(solution)/shard_map/broadcast_in_dim | solution.py:39
  305.0 31.3 %fusion.100 = f32[16,48,3,3,3]{1,0,4,3,2:T(8,128)} fusion(bf16[48,1,18,4,130]{0,1,4,3,2:T(2,128)(2,1)} %copy.230, bf16[16,1,16,2,128]{0,1,4,3,2:T(2,128)(2,1)} %copy.231), kind=kOutput, calls=%fused_computation.139 | convolution fusion | flops 169869312 | bytes 1112576 | tf_op jit(solution)/shard_map/transpose | solution.py:46
  336.3 0.8 copy.235
  337.1 293.2 %all-reduce.6.cloned.1.call-done = f32[16,48,3,3,3]{1,0,4,3,2:T(8,128)} async-done(((f32[16,48,3,3,3]{1,0,4,3,2:T(8,128)}), f32[16,48,3,3,3]{1,0,4,3,2:T(8,128)}) %all-reduce.6.cloned.1.call-update) | async-done | bytes 82960 | tf_op jit(solution)/shard_map/psum | solution.py:116
  630.3 1.6 broadcast_multiply_fusion.1
  (91 shorter events, 8.5 us)
Async XLA Ops:
  7.2 47.5 %copy-start = (bf16[16,48,3,3,3]{1,0,4,3,2:T(8,128)(2,1)S(1)}, bf16[16,48,3,3,3]{1,0,4,3,2:T(8,128)(2,1)}, u32[]{:S(2)}) copy-start(bf16[16,48,3,3,3]{1,0,4,3,2:T(8,128)(2,1)} %param.7) | copy-start | bytes 124420
  7.2 13.4 %copy-start.4 = (bf16[16,16,2,128]{3,2,1,0:T(2,128)(2,1)S(1)}, bf16[16,16,2,128]{3,2,1,0:T(2,128)(2,1)}, u32[]{:S(2)}) copy-start(bf16[16,16,2,128]{3,2,1,0:T(2,128)(2,1)} %param.5) | copy-start | bytes 393220
  7.2 34.1 %copy-start.5 = (bf16[16,16,2,128]{3,2,1,0:T(2,128)(2,1)S(1)}, bf16[16,16,2,128]{3,2,1,0:T(2,128)(2,1)}, u32[]{:S(2)}) copy-start(bf16[16,16,2,128]{3,2,1,0:T(2,128)(2,1)} %param.4) | copy-start | bytes 393220
  8.0 12.6 %collective-permute-start.6 = (bf16[16,1,2,128]{3,2,1,0:T(2,128)(2,1)S(1)}, bf16[16,1,2,128]{3,2,1,0:T(2,128)(2,1)S(1)}, u32[]{:S(2)}, u32[]{:S(2)}) collective-permute-start(bf16[16,1,2,128]{3,2,1,0:T(2,128)(2,1)S(1)} %get-tuple-element.39), channel_id=1, source_target_pairs={{0,8},{8,16},{16,24},{24,32},{32,40},{40,48},{48,56},{56,64},{64,7... | collective-permute-start | bytes 24584 | tf_op jit(solution)/shard_map/ppermute | solution.py:15
  12.6 8.1 %collective-permute-start.7 = (bf16[16,1,2,128]{3,2,1,0:T(2,128)(2,1)S(1)}, bf16[16,1,2,128]{3,2,1,0:T(2,128)(2,1)S(1)}, u32[]{:S(2)}, u32[]{:S(2)}) collective-permute-start(bf16[16,1,2,128]{3,2,1,0:T(2,128)(2,1)S(1)} %get-tuple-element.38), channel_id=1, source_target_pairs={{8,0},{16,8},{24,16},{32,24},{40,32},{48,40},{56,48},{64,56},{72,6... | collective-permute-start | bytes 24584 | tf_op jit(solution)/shard_map/ppermute | solution.py:16
  21.0 24.1 %collective-permute-start.9 = (bf16[16,18,2,1]{3,2,1,0:T(2,128)(2,1)S(1)}, bf16[16,18,2,1]{3,2,1,0:T(2,128)(2,1)S(1)}, u32[]{:S(2)}, u32[]{:S(2)}) collective-permute-start(bf16[16,18,2,1]{3,2,1,0:T(2,128)(2,1)S(1)} %get-tuple-element.37), channel_id=1, source_target_pairs={{1,0},{2,1},{3,2},{4,3},{5,4},{6,5},{7,6},{9,8},{10,9},{11,10},{12... | collective-permute-start | bytes 3464 | tf_op jit(solution)/shard_map/ppermute | solution.py:16
  22.3 22.8 %collective-permute-start.8 = (bf16[16,18,2,1]{3,2,1,0:T(2,128)(2,1)S(1)}, bf16[16,18,2,1]{3,2,1,0:T(2,128)(2,1)S(1)}, u32[]{:S(2)}, u32[]{:S(2)}) collective-permute-start(bf16[16,18,2,1]{3,2,1,0:T(2,128)(2,1)S(1)} %get-tuple-element.36), channel_id=1, source_target_pairs={{0,1},{1,2},{2,3},{3,4},{4,5},{5,6},{6,7},{8,9},{9,10},{10,11},{11... | collective-permute-start | bytes 3464 | tf_op jit(solution)/shard_map/ppermute | solution.py:15
  31.3 31.1 %all-to-all-start = ((bf16[8,2,512]{2,1,0:T(2,128)(2,1)}), bf16[8,2,512]{2,1,0:T(2,128)(2,1)S(1)}, u32[]{:S(2)}, u32[]{:S(2)}) async-start(bf16[8,2,512]{2,1,0:T(2,128)(2,1)} %reshape.289), calls=%async_computation | async-start | bytes 32768 | tf_op jit(solution)/shard_map/all_to_all | solution.py:84
  48.5 6.2 copy-start.10
  62.6 32.4 %collective-permute-start.1 = (bf16[16,1,1,512]{3,0,2,1:T(8,128)(2,1)S(1)}, bf16[16,1,1,512]{3,0,2,1:T(8,128)(2,1)S(1)}, u32[]{:S(2)}, u32[]{:S(2)}) collective-permute-start(bf16[16,1,1,512]{3,0,2,1:T(8,128)(2,1)S(1)} %all_to_all.11), channel_id=1, source_target_pairs={{1,0},{2,1},{3,2},{4,3},{5,4},{6,5},{7,6},{8,7},{9,8},{10,9},{11,1... | collective-permute-start | bytes 49160 | tf_op jit(solution)/shard_map/ppermute | solution.py:16
  71.1 23.9 %collective-permute-start = (bf16[16,1,1,512]{3,0,2,1:T(8,128)(2,1)S(1)}, bf16[16,1,1,512]{3,0,2,1:T(8,128)(2,1)}, u32[]{:S(2)}, u32[]{:S(2)}) collective-permute-start(bf16[16,1,1,512]{3,0,2,1:T(8,128)(2,1)S(1)} %all_to_all.11), channel_id=1, source_target_pairs={{0,1},{1,2},{2,3},{3,4},{4,5},{5,6},{6,7},{7,8},{8,9},{9,10},{10,1... | collective-permute-start | bytes 49160 | tf_op jit(solution)/shard_map/ppermute | solution.py:15
  78.6 22.7 %all-to-all-start.2 = ((bf16[8,2,1024]{2,1,0:T(2,128)(2,1)}), bf16[8,2,1024]{2,1,0:T(2,128)(2,1)S(1)}, u32[]{:S(2)}, u32[]{:S(2)}) async-start(bf16[8,2,1024]{2,1,0:T(2,128)(2,1)} %reshape.287), calls=%async_computation.2 | async-start | bytes 65536 | tf_op jit(solution)/shard_map/all_to_all | solution.py:84
  92.2 4.7 copy-start.8
  92.2 4.7 copy-start.9
  101.6 136.7 %collective-permute-start.11 = (bf16[32,1,1,512]{3,0,2,1:T(8,128)(2,1)S(1)}, bf16[32,1,1,512]{3,0,2,1:T(8,128)(2,1)S(1)}, u32[]{:S(2)}, u32[]{:S(2)}) collective-permute-start(bf16[32,1,1,512]{3,0,2,1:T(8,128)(2,1)S(1)} %get-tuple-element.40), channel_id=1, source_target_pairs={{1,0},{2,1},{3,2},{4,3},{5,4},{6,5},{7,6},{8,7},{9,8},{10,9},{11,1... | collective-permute-start | bytes 98312 | tf_op jit(solution)/shard_map/ppermute | solution.py:16
  109.7 128.6 %collective-permute-start.10 = (bf16[32,1,1,512]{3,0,2,1:T(8,128)(2,1)S(1)}, bf16[32,1,1,512]{3,0,2,1:T(8,128)(2,1)S(1)}, u32[]{:S(2)}, u32[]{:S(2)}) collective-permute-start(bf16[32,1,1,512]{3,0,2,1:T(8,128)(2,1)S(1)} %get-tuple-element.40), channel_id=1, source_target_pairs={{0,1},{1,2},{2,3},{3,4},{4,5},{5,6},{6,7},{7,8},{8,9},{9,10},{10,1... | collective-permute-start | bytes 98312 | tf_op jit(solution)/shard_map/ppermute | solution.py:15
  114.7 129.9 %all-to-all-start.1 = ((bf16[8,2,1024]{2,1,0:T(2,128)(2,1)}), bf16[8,2,1024]{2,1,0:T(2,128)(2,1)S(1)}, u32[]{:S(2)}, u32[]{:S(2)}) async-start(bf16[8,2,1024]{2,1,0:T(2,128)(2,1)} %reshape.291), calls=%async_computation.1 | async-start | bytes 65536 | tf_op jit(solution)/shard_map/all_to_all | solution.py:92
  240.7 1.3 copy-start.7
  244.6 12.2 %all-to-all-start.3 = ((bf16[8,2,512]{2,1,0:T(2,128)(2,1)}), bf16[8,2,512]{2,1,0:T(2,128)(2,1)S(1)}, u32[]{:S(2)}, u32[]{:S(2)}) async-start(bf16[8,2,512]{2,1,0:T(2,128)(2,1)} %reshape.293), calls=%async_computation.3 | async-start | bytes 32768 | tf_op jit(solution)/shard_map/all_to_all | solution.py:92
  247.9 382.4 %all-reduce.6.cloned.1.call-start = ((), (), s32[]{:S(2)}) async-start(), calls=%async_computation.4 | async-start | bytes 442368 | tf_op jit(solution)/shard_map/psum | solution.py:116
  248.9 9.2 %collective-permute-start.3 = (bf16[48,1,2,128]{3,0,2,1:T(8,128)(2,1)S(1)}, bf16[48,1,2,128]{3,0,2,1:T(8,128)(2,1)S(1)}, u32[]{:S(2)}, u32[]{:S(2)}) collective-permute-start(bf16[48,1,2,128]{3,0,2,1:T(8,128)(2,1)S(1)} %get-tuple-element.35), channel_id=1, source_target_pairs={{8,0},{16,8},{24,16},{32,24},{40,32},{48,40},{56,48},{64,56},{72,6... | collective-permute-start | bytes 73736 | tf_op jit(solution)/shard_map/ppermute | solution.py:16
  251.8 6.3 collective-permute-start.2
  257.3 10.6 %copy-start.3 = (f32[16,2,1,136,16]{3,4,1,0,2:T(8,128)S(1)}, f32[16,2,1,136,16]{3,4,1,0,2:T(8,128)}, u32[]{:S(2)}) copy-start(f32[16,2,1,136,16]{3,4,1,0,2:T(8,128)} %reshape.252) | copy-start | bytes 835588
  258.3 15.9 %collective-permute-start.5 = (bf16[48,18,2,1]{3,0,2,1:T(8,128)(2,1)S(1)}, bf16[48,18,2,1]{3,0,2,1:T(8,128)(2,1)S(1)}, u32[]{:S(2)}, u32[]{:S(2)}) collective-permute-start(bf16[48,18,2,1]{3,0,2,1:T(8,128)(2,1)S(1)} %get-tuple-element.33), channel_id=1, source_target_pairs={{1,0},{2,1},{3,2},{4,3},{5,4},{6,5},{7,6},{9,8},{10,9},{11,10},{12... | collective-permute-start | bytes 10376 | tf_op jit(solution)/shard_map/ppermute | solution.py:16
  259.6 15.6 %collective-permute-start.4 = (bf16[48,18,2,1]{3,0,2,1:T(8,128)(2,1)S(1)}, bf16[48,18,2,1]{3,0,2,1:T(8,128)(2,1)S(1)}, u32[]{:S(2)}, u32[]{:S(2)}) collective-permute-start(bf16[48,18,2,1]{3,0,2,1:T(8,128)(2,1)S(1)} %get-tuple-element.32), channel_id=1, source_target_pairs={{0,1},{1,2},{2,3},{3,4},{4,5},{5,6},{6,7},{8,9},{9,10},{10,11},{11... | collective-permute-start | bytes 10376 | tf_op jit(solution)/shard_map/ppermute | solution.py:15
  275.2 0.8 copy-start.1
  284.5 9.3 %copy-start.6 = (pred[8,17]{1,0:T(8,128)(4,1)S(1)}, pred[8,17]{1,0:T(8,128)(4,1)}, u32[]{:S(2)}) copy-start(pred[8,17]{1,0:T(8,128)(4,1)} %constant.46) | copy-start | bytes 412
  293.8 1.3 copy-start.2
Sparse Core Ops, SparseCore 0:
  336.4 293.8 all-reduce.5
where the time goes:
time: 648 us; the launch traced here: 639 us
  waiting for transfers between devices  302 us (47%)
  blocking collectives  106 us (16%)
  starting transfers between devices  90.7 us (14%)
  local copies, waits for them, and re-layouts  56.7 us (9%)
  matrix products  50.9 us (8%)
  other arithmetic  18 us (3%)
  between operations  14.9 us (2%)
    psum x1, waiting for transfers between devices, shards(): lax.psum((local_fine, local_coarse), ('wide', 'narrow'))  293 us
    psum x1, blocking collectives, shards(): lax.psum((local_fine, local_coarse), ('wide', 'narrow'))  106 us
    transpose x2, matrix products, weight_grad(): return jnp.transpose(result, (1, 0, 2, 3, 4))  37 us
    ppermute x6, starting transfers between devices, extended_2(): before = lax.ppermute(last, axis, up)  27.7 us
    ppermute x6, starting transfers between devices, extended_2(): after = lax.ppermute(first, axis, down)  27.6 us
    conv_general_dilated x19, local copies, waits for them, and re-layouts, correlate(): lax.conv_general_dilated(padded[None], kernel, (1, 1, 1), 'VALID', dimens...  23.1 us
    all_to_all x2, starting transfers between devices, into_coarse(): lax.all_to_all(shortened(field), 'narrow', split_axis=1, concat_axis=3, t...  20.8 us
    all_to_all x2, starting transfers between devices, into_fine(): lax.all_to_all(shortened(field), 'narrow', split_axis=3, concat_axis=1, t...  14.5 us
  transfers between devices with their start and end apart: 17, of which 4 were waited for; matrix products, arithmetic and copies ran while one was open for 10% of the time, Pallas kernels for 0%

commit v1 on v0

--- a/solution.py
+++ b/solution.py
@@ -113,7 +113,7 @@
     grad_features = (
         grad_joined[:channels] + upsample(into_fine(grad_pooled)).astype(jnp.float32) / 8.0
     ).astype(jnp.bfloat16)
-    fine_total, coarse_total = lax.psum((local_fine, local_coarse), ("wide", "narrow"))
+    fine_total, coarse_total = lax.psum(lax.psum((local_fine, local_coarse), "wide"), "narrow")
     all_cells = (
         features.shape[1]
         * features.shape[2]

time: 648 us -> 1200 us (1.85)
  waiting for transfers between devices: 302 us -> 604 us
  blocking collectives: 106 us -> 340 us
    psum x1 -> x2, waiting for transfers between devices: 293 us -> 599 us  [the longest x1 492 us: shards(): lax.psum((local_fine, local_coarse), 'wide')]
    psum x1 -> x2, blocking collectives: 106 us -> 340 us  [the longest x1 261 us: shards(): lax.psum((local_fine, local_coarse), 'wide')]
    ppermute x6, starting transfers between devices: 27.6 us -> 39.9 us  [extended_2(): after = lax.ppermute(first, axis, down)]
  transfers between devices with their start and end apart: 17 -> 18, of which waited for: 4 -> 4; matrix products, arithmetic and copies ran while one was open for 10% -> 6% of each run, Pallas kernels for 0% -> 0%
where the time goes in v1:
time: 1200 us; the launch traced here: 1190 us
  waiting for transfers between devices  604 us (50%)
  blocking collectives  340 us (28%)
  starting transfers between devices  102 us (8%)
  local copies, waits for them, and re-layouts  58.4 us (5%)
  matrix products  51.6 us (4%)
  other arithmetic  21.1 us (2%)
  between operations  15.1 us (1%)
    psum x1, waiting for transfers between devices, shards(): lax.psum((local_fine, local_coarse), 'wide')  492 us
    psum x1, blocking collectives, shards(): lax.psum((local_fine, local_coarse), 'wide')  261 us
    psum x1, waiting for transfers between devices, shards(): lax.psum(lax.psum((local_fine, local_coarse), 'wide'), 'narrow')  107 us
    psum x1, blocking collectives, shards(): lax.psum(lax.psum((local_fine, local_coarse), 'wide'), 'narrow')  79.1 us
    ppermute x6, starting transfers between devices, extended_2(): after = lax.ppermute(first, axis, down)  39.9 us
    transpose x2, matrix products, weight_grad(): return jnp.transpose(result, (1, 0, 2, 3, 4))  37.7 us
    ppermute x6, starting transfers between devices, extended_2(): before = lax.ppermute(last, axis, up)  26.8 us
  transfers between devices with their start and end apart: 18, of which 4 were waited for; matrix products, arithmetic and copies ran while one was open for 6% of the time, Pallas kernels for 0%

profile of v1, /device:TPU:1, one launch (start us, length us, event | category | flops | bytes accessed | tf_op | source)
XLA Modules:
  0.0 1191.7 jit_solution(4838750973193352397)
XLA Ops:
  7.2 0.8 fusion.97
  8.0 4.6 collective-permute-start.6
  12.6 5.5 collective-permute-start.7
  18.1 1.3 convert_reduce_fusion
  19.7 0.9 reduce_sum.25
  21.0 1.3 collective-permute-start.9
  22.3 8.1 collective-permute-start.8
  31.3 10.0 all-to-all-start
  41.3 3.8 copy.231
  45.1 1.3 fusion.54
  46.7 1.8 reshape.286
  48.6 5.0 copy.219
  53.6 1.0 slice.64
  54.7 5.0 fusion.26
  60.3 2.0 copy.221
  62.6 8.5 collective-permute-start.1
  71.1 2.2 collective-permute-start
  73.3 1.9 slice_reduce_fusion
  75.2 1.8 reduce_sum.37
  76.9 1.0 copy.222
  78.7 10.8 all-to-all-start.2
  89.5 2.8 copy.220
  92.3 2.1 reshape.252
  94.5 0.8 fusion.98
  95.6 0.8 copy.204
  96.4 1.2 fusion.46
  97.6 0.8 fusion.99
  98.7 2.0 copy.233
  101.0 8.2 collective-permute-start.11
  109.2 1.9 collective-permute-start.10
  112.5 2.1 reduce.8
  114.6 1.7 reshape.291
  116.3 11.2 all-to-all-start.1
  127.4 0.9 fusion.74
  128.5 6.4 fusion.101
  134.9 260.6 %psum.30 = f32[32,16,3,3,3]{0,1,4,3,2:T(8,128)S(1)} all-reduce(f32[32,16,3,3,3]{0,1,4,3,2:T(8,128)} %fusion.101), channel_id=1, replica_groups=mesh['wide'=64,'narrow'=8] {'wide'}, use_global_device_ids=true, to_apply=%region_6.7 | all-reduce | flops 13824 | bytes 110592 | tf_op jit(solution)/shard_map/psum | solution.py:116
  395.5 79.1 %psum.31 = f32[32,16,3,3,3]{0,1,4,3,2:T(8,128)S(1)} all-reduce(f32[32,16,3,3,3]{0,1,4,3,2:T(8,128)S(1)} %psum.30), channel_id=1, replica_groups=mesh['wide'=64,'narrow'=8] {'narrow'}, use_global_device_ids=true, to_apply=%region_7.8 | all-reduce | flops 13824 | bytes 110592 | tf_op jit(solution)/shard_map/psum | solution.py:116
  475.4 0.9 fusion.55
  476.9 1.7 copy.225
  478.6 1.1 fusion.33
  480.2 1.4 reduce.9
  481.6 0.8 reshape.293
  482.3 3.3 all-to-all-start.3
  485.7 0.9 reshape.292
  487.4 15.2 %collective-permute-start.3 = (bf16[48,1,2,128]{3,0,2,1:T(8,128)(2,1)S(1)}, bf16[48,1,2,128]{3,0,2,1:T(8,128)(2,1)S(1)}, u32[]{:S(2)}, u32[]{:S(2)}) collective-permute-start(bf16[48,1,2,128]{3,0,2,1:T(8,128)(2,1)S(1)} %get-tuple-element.35), channel_id=1, source_target_pairs={{8,0},{16,8},{24,16},{32,24},{40,32},{48,40},{56,48},{64,56},{72,6... | collective-permute-start | bytes 73736 | tf_op jit(solution)/shard_map/ppermute | solution.py:16
  502.6 1.9 collective-permute-start.2
  506.0 1.3 collective-permute-start.5
  507.3 8.1 collective-permute-start.4
  515.4 0.8 copy.236
  516.2 2.9 collective-permute-done.5
  519.1 1.5 collective-permute-done.4
  520.6 0.8 copy-done.2
  521.3 2.0 fusion.111
  523.3 4.9 copy.240
  528.2 1.3 pad.22.clone
  529.9 6.5 fusion.9
  536.4 2.7 copy.214
  539.2 2.1 fusion.110
  541.3 8.8 copy.230
  550.2 31.3 %fusion.100 = f32[16,48,3,3,3]{1,0,4,3,2:T(8,128)} fusion(bf16[48,1,18,4,130]{0,1,4,3,2:T(2,128)(2,1)} %copy.230, bf16[16,1,16,2,128]{0,1,4,3,2:T(2,128)(2,1)} %copy.231), kind=kOutput, calls=%fused_computation.139 | convolution fusion | flops 169869312 | bytes 1112576 | tf_op jit(solution)/shard_map/transpose | solution.py:46
  582.9 492.1 %all-reduce.7.cloned.1.call-done = f32[16,48,3,3,3]{1,0,4,3,2:T(8,128)} async-done(((f32[16,48,3,3,3]{1,0,4,3,2:T(8,128)}), f32[16,48,3,3,3]{1,0,4,3,2:T(8,128)}) %all-reduce.7.cloned.1.call-update) | async-done | bytes 82960 | tf_op jit(solution)/shard_map/psum | solution.py:116
  1075.0 0.8 copy.235
  1075.8 107.1 %all-reduce.9.cloned.1.call-done = f32[16,48,3,3,3]{1,0,4,3,2:T(8,128)} async-done(((f32[16,48,3,3,3]{1,0,4,3,2:T(8,128)}), f32[16,48,3,3,3]{1,0,4,3,2:T(8,128)}) %all-reduce.9.cloned.1.call-update) | async-done | bytes 82960 | tf_op jit(solution)/shard_map/psum | solution.py:116
  1182.9 1.6 broadcast_multiply_fusion.1
  (95 shorter events, 11.7 us)
Async XLA Ops:
  7.2 47.5 %copy-start = (bf16[16,48,3,3,3]{1,0,4,3,2:T(8,128)(2,1)S(1)}, bf16[16,48,3,3,3]{1,0,4,3,2:T(8,128)(2,1)}, u32[]{:S(2)}) copy-start(bf16[16,48,3,3,3]{1,0,4,3,2:T(8,128)(2,1)} %param.7) | copy-start | bytes 124420
  7.2 13.4 %copy-start.3 = (bf16[16,16,2,128]{3,2,1,0:T(2,128)(2,1)S(1)}, bf16[16,16,2,128]{3,2,1,0:T(2,128)(2,1)}, u32[]{:S(2)}) copy-start(bf16[16,16,2,128]{3,2,1,0:T(2,128)(2,1)} %param.5) | copy-start | bytes 393220
  7.2 34.1 %copy-start.4 = (bf16[16,16,2,128]{3,2,1,0:T(2,128)(2,1)S(1)}, bf16[16,16,2,128]{3,2,1,0:T(2,128)(2,1)}, u32[]{:S(2)}) copy-start(bf16[16,16,2,128]{3,2,1,0:T(2,128)(2,1)} %param.4) | copy-start | bytes 393220
  8.0 12.6 %collective-permute-start.6 = (bf16[16,1,2,128]{3,2,1,0:T(2,128)(2,1)S(1)}, bf16[16,1,2,128]{3,2,1,0:T(2,128)(2,1)S(1)}, u32[]{:S(2)}, u32[]{:S(2)}) collective-permute-start(bf16[16,1,2,128]{3,2,1,0:T(2,128)(2,1)S(1)} %get-tuple-element.39), channel_id=1, source_target_pairs={{0,8},{8,16},{16,24},{24,32},{32,40},{40,48},{48,56},{56,64},{64,7... | collective-permute-start | bytes 24584 | tf_op jit(solution)/shard_map/ppermute | solution.py:15
  12.6 8.1 collective-permute-start.7
  21.0 24.1 %collective-permute-start.9 = (bf16[16,18,2,1]{3,2,1,0:T(2,128)(2,1)S(1)}, bf16[16,18,2,1]{3,2,1,0:T(2,128)(2,1)S(1)}, u32[]{:S(2)}, u32[]{:S(2)}) collective-permute-start(bf16[16,18,2,1]{3,2,1,0:T(2,128)(2,1)S(1)} %get-tuple-element.37), channel_id=1, source_target_pairs={{1,0},{2,1},{3,2},{4,3},{5,4},{6,5},{7,6},{9,8},{10,9},{11,10},{12... | collective-permute-start | bytes 3464 | tf_op jit(solution)/shard_map/ppermute | solution.py:16
  22.3 22.8 %collective-permute-start.8 = (bf16[16,18,2,1]{3,2,1,0:T(2,128)(2,1)S(1)}, bf16[16,18,2,1]{3,2,1,0:T(2,128)(2,1)S(1)}, u32[]{:S(2)}, u32[]{:S(2)}) collective-permute-start(bf16[16,18,2,1]{3,2,1,0:T(2,128)(2,1)S(1)} %get-tuple-element.36), channel_id=1, source_target_pairs={{0,1},{1,2},{2,3},{3,4},{4,5},{5,6},{6,7},{8,9},{9,10},{10,11},{11... | collective-permute-start | bytes 3464 | tf_op jit(solution)/shard_map/ppermute | solution.py:15
  31.3 31.1 %all-to-all-start = ((bf16[8,2,512]{2,1,0:T(2,128)(2,1)}), bf16[8,2,512]{2,1,0:T(2,128)(2,1)S(1)}, u32[]{:S(2)}, u32[]{:S(2)}) async-start(bf16[8,2,512]{2,1,0:T(2,128)(2,1)} %reshape.289), calls=%async_computation | async-start | bytes 32768 | tf_op jit(solution)/shard_map/all_to_all | solution.py:84
  48.5 6.1 copy-start.10
  62.6 31.9 %collective-permute-start.1 = (bf16[16,1,1,512]{3,0,2,1:T(8,128)(2,1)S(1)}, bf16[16,1,1,512]{3,0,2,1:T(8,128)(2,1)S(1)}, u32[]{:S(2)}, u32[]{:S(2)}) collective-permute-start(bf16[16,1,1,512]{3,0,2,1:T(8,128)(2,1)S(1)} %all_to_all.11), channel_id=1, source_target_pairs={{1,0},{2,1},{3,2},{4,3},{5,4},{6,5},{7,6},{8,7},{9,8},{10,9},{11,1... | collective-permute-start | bytes 49160 | tf_op jit(solution)/shard_map/ppermute | solution.py:16
  71.1 23.4 %collective-permute-start = (bf16[16,1,1,512]{3,0,2,1:T(8,128)(2,1)S(1)}, bf16[16,1,1,512]{3,0,2,1:T(8,128)(2,1)}, u32[]{:S(2)}, u32[]{:S(2)}) collective-permute-start(bf16[16,1,1,512]{3,0,2,1:T(8,128)(2,1)S(1)} %all_to_all.11), channel_id=1, source_target_pairs={{0,1},{1,2},{2,3},{3,4},{4,5},{5,6},{6,7},{7,8},{8,9},{9,10},{10,1... | collective-permute-start | bytes 49160 | tf_op jit(solution)/shard_map/ppermute | solution.py:15
  78.7 22.1 %all-to-all-start.2 = ((bf16[8,2,1024]{2,1,0:T(2,128)(2,1)}), bf16[8,2,1024]{2,1,0:T(2,128)(2,1)S(1)}, u32[]{:S(2)}, u32[]{:S(2)}) async-start(bf16[8,2,1024]{2,1,0:T(2,128)(2,1)} %reshape.287), calls=%async_computation.2 | async-start | bytes 65536 | tf_op jit(solution)/shard_map/all_to_all | solution.py:84
  92.3 4.1 copy-start.7
  92.3 4.1 copy-start.9
  101.0 374.3 %collective-permute-start.11 = (bf16[32,1,1,512]{3,0,2,1:T(8,128)(2,1)S(1)}, bf16[32,1,1,512]{3,0,2,1:T(8,128)(2,1)}, u32[]{:S(2)}, u32[]{:S(2)}) collective-permute-start(bf16[32,1,1,512]{3,0,2,1:T(8,128)(2,1)S(1)} %get-tuple-element.40), channel_id=1, source_target_pairs={{1,0},{2,1},{3,2},{4,3},{5,4},{6,5},{7,6},{8,7},{9,8},{10,9},{11,1... | collective-permute-start | bytes 98312 | tf_op jit(solution)/shard_map/ppermute | solution.py:16
  109.2 366.1 %collective-permute-start.10 = (bf16[32,1,1,512]{3,0,2,1:T(8,128)(2,1)S(1)}, bf16[32,1,1,512]{3,0,2,1:T(8,128)(2,1)}, u32[]{:S(2)}, u32[]{:S(2)}) collective-permute-start(bf16[32,1,1,512]{3,0,2,1:T(8,128)(2,1)S(1)} %get-tuple-element.40), channel_id=1, source_target_pairs={{0,1},{1,2},{2,3},{3,4},{4,5},{5,6},{6,7},{7,8},{8,9},{9,10},{10,1... | collective-permute-start | bytes 98312 | tf_op jit(solution)/shard_map/ppermute | solution.py:15
  116.3 366.1 %all-to-all-start.1 = ((bf16[8,2,1024]{2,1,0:T(2,128)(2,1)}), bf16[8,2,1024]{2,1,0:T(2,128)(2,1)}, u32[]{:S(2)}, u32[]{:S(2)}) async-start(bf16[8,2,1024]{2,1,0:T(2,128)(2,1)} %reshape.291), calls=%async_computation.1 | async-start | bytes 65536 | tf_op jit(solution)/shard_map/all_to_all | solution.py:92
  395.5 83.1 %copy-start.8 = (bf16[32,16,3,3,3]{0,1,4,3,2:T(8,128)(2,1)S(1)}, bf16[32,16,3,3,3]{0,1,4,3,2:T(8,128)(2,1)}, u32[]{:S(2)}) copy-start(bf16[32,16,3,3,3]{0,1,4,3,2:T(8,128)(2,1)} %param.6) | copy-start | bytes 82948
  478.6 1.3 copy-start.6
  482.3 22.2 %all-to-all-start.3 = ((bf16[8,2,512]{2,1,0:T(2,128)(2,1)}), bf16[8,2,512]{2,1,0:T(2,128)(2,1)S(1)}, u32[]{:S(2)}, u32[]{:S(2)}) async-start(bf16[8,2,512]{2,1,0:T(2,128)(2,1)} %reshape.293), calls=%async_computation.3 | async-start | bytes 32768 | tf_op jit(solution)/shard_map/all_to_all | solution.py:92
  485.7 589.2 %all-reduce.7.cloned.1.call-start = ((), (), s32[]{:S(2)}) async-start(), calls=%async_computation.4 | async-start | bytes 442368 | tf_op jit(solution)/shard_map/psum | solution.py:116
  487.4 18.4 %collective-permute-start.3 = (bf16[48,1,2,128]{3,0,2,1:T(8,128)(2,1)S(1)}, bf16[48,1,2,128]{3,0,2,1:T(8,128)(2,1)S(1)}, u32[]{:S(2)}, u32[]{:S(2)}) collective-permute-start(bf16[48,1,2,128]{3,0,2,1:T(8,128)(2,1)S(1)} %get-tuple-element.35), channel_id=1, source_target_pairs={{8,0},{16,8},{24,16},{32,24},{40,32},{48,40},{56,48},{64,56},{72,6... | collective-permute-start | bytes 73736 | tf_op jit(solution)/shard_map/ppermute | solution.py:16
  502.6 3.2 collective-permute-start.2
  506.0 13.1 %collective-permute-start.5 = (bf16[48,18,2,1]{3,0,2,1:T(8,128)(2,1)S(1)}, bf16[48,18,2,1]{3,0,2,1:T(8,128)(2,1)S(1)}, u32[]{:S(2)}, u32[]{:S(2)}) collective-permute-start(bf16[48,18,2,1]{3,0,2,1:T(8,128)(2,1)S(1)} %get-tuple-element.33), channel_id=1, source_target_pairs={{1,0},{2,1},{3,2},{4,3},{5,4},{6,5},{7,6},{9,8},{10,9},{11,10},{12... | collective-permute-start | bytes 10376 | tf_op jit(solution)/shard_map/ppermute | solution.py:16
  507.3 13.3 %collective-permute-start.4 = (bf16[48,18,2,1]{3,0,2,1:T(8,128)(2,1)S(1)}, bf16[48,18,2,1]{3,0,2,1:T(8,128)(2,1)S(1)}, u32[]{:S(2)}, u32[]{:S(2)}) collective-permute-start(bf16[48,18,2,1]{3,0,2,1:T(8,128)(2,1)S(1)} %get-tuple-element.32), channel_id=1, source_target_pairs={{0,1},{1,2},{2,3},{3,4},{4,5},{5,6},{6,7},{8,9},{9,10},{10,11},{11... | collective-permute-start | bytes 10376 | tf_op jit(solution)/shard_map/ppermute | solution.py:15
  519.1 1.5 copy-start.1
  520.6 0.8 copy-start.2
  550.2 31.4 %copy-start.5 = (pred[8,17]{1,0:T(8,128)(4,1)S(1)}, pred[8,17]{1,0:T(8,128)(4,1)}, u32[]{:S(2)}) copy-start(pred[8,17]{1,0:T(8,128)(4,1)} %constant.46) | copy-start | bytes 412
  581.5 601.3 %all-reduce.9.cloned.1.call-start = ((), (), s32[]{:S(2)}) async-start(), calls=%async_computation.5 | async-start | bytes 442368 | tf_op jit(solution)/shard_map/psum | solution.py:116
Sparse Core Ops, SparseCore 0:
  581.6 493.2 all-reduce.6
  1078.1 104.6 all-reduce.8
